TPU v7x, 32 devices: a whole 2x2x4 slice. The times are simulated.
32 devices in a mesh: tm: 8 (over z, x), seq: 2 (over y), mp: 2 (over core).
Axes of the slice: x: 2, y: 2, z: 4, core: 2. Of those that a mesh axis runs over, the one named last changes fastest.
Arguments:
- student_q: bfloat16 [2, 1024, 5120], P('seq', 'tm', 'mp'), may hold values from -110 to 110
- student_k: bfloat16 [2, 1024, 5120], P('seq', 'tm', 'mp'), may hold values from -6 to 6
- student_v: bfloat16 [2, 1024, 5120], P('seq', 'tm', 'mp'), may hold values from -6 to 6
- teacher_q: bfloat16 [2, 1024, 5120], P('seq', 'tm', 'mp'), may hold values from -110 to 110
- teacher_k: bfloat16 [2, 1024, 5120], P('seq', 'tm', 'mp'), may hold values from -6 to 6
- stagger: int32 [2], P('seq'), may hold values from 0 to 4, as said below
- clip_lengths: int32 [2, 3], P('seq'), may hold values from 1 to 5, 8 in all within a row
Outputs:
- generated: bfloat16 [2, 1024, 5120], P('seq', 'tm', 'mp')
- score_rows: bfloat16 [2, 1024, 5120], P('seq', 'tm', 'mp')
Inputs may be any that keep to these rules, and one draw needn't show every extreme that they name: `clip_lengths`: the lengths of each video sum to 8, and some clip has 5 blocks. `stagger`: some video has the value 8 // 2.
All inputs are finite; a program needn't handle non-finite values.
Results may differ from a plain program's by a relative error of at most 0.007.
Values may be sent and summed in bfloat16 or wider, within the bound.
No kernel may reach another device: no remote copies, remote signals or barrier semaphores. Data moves between devices by JAX's collectives and lax.ppermute only.
A program may use at most 64 MiB of HBM per device.

v0:
```python
import functools
import math

import jax
import jax.numpy as jnp
from jax import lax
from jax.experimental import pallas as pl
from jax.experimental.pallas import tpu as pltpu
from jax.sharding import PartitionSpec as P

HD = 128
TOK = 128
NEG = -1e30
RATE = math.log2(math.e) / math.sqrt(HD)
MIB = 2**20
VMEM = pl.BlockSpec(memory_space=pltpu.VMEM)
SMEM = pl.BlockSpec(memory_space=pltpu.SMEM)
WHOLE = pltpu.CompilerParams(vmem_limit_bytes=60 * MIB)
LOCAL = pltpu.CompilerParams(vmem_limit_bytes=24 * MIB)


def attend(q, k, v, bias):
    g = q.shape[0]
    scores = lax.dot_general(
        q.reshape(g * TOK, HD), k, (((1,), (1,)), ((), ())), preferred_element_type=jnp.float32
    )
    scores = scores.reshape(g, TOK, -1) + bias
    top = jnp.max(scores, axis=-1, keepdims=True)
    weights = jnp.exp2((scores - top) * RATE)
    total = jnp.sum(weights, axis=-1, keepdims=True)
    weights = weights.astype(jnp.bfloat16).reshape(g * TOK, -1)
    mixed = jnp.dot(weights, v, preferred_element_type=jnp.float32)
    return mixed.reshape(g, TOK, HD) / total


def student_head(pairs, first, sources, o_ref, o_at):
    (q_ref, q_at), (k_ref, k_at), (v_ref, v_at) = sources
    for i in pairs:
        width = (i + 2) * TOK
        block = lax.broadcasted_iota(jnp.int32, (2, 1, width), 2) // TOK
        own = lax.broadcasted_iota(jnp.int32, (2, 1, width), 0) + i
        bias = jnp.where((block == own) | (block >= first) & (block < own), 0.0, NEG)
        k = k_ref[0 : i + 2, k_at].reshape(width, HD)
        v = v_ref[0 : i + 2, v_at].reshape(width, HD)
        o_ref[i : i + 2, o_at] = attend(q_ref[i : i + 2, q_at], k, v, bias).astype(jnp.bfloat16)


def teacher_head(blocks, rows, clip_ref, sources, gen, o_ref, o_at):
    (q_ref, q_at), (k_ref, k_at) = sources
    reach = blocks // 2 + 1
    width = reach * TOK
    offset = lax.broadcasted_iota(jnp.int32, (1, 1, width), 2) // TOK
    for i in rows:
        low = clip_ref[0, i]
        high = clip_ref[1, i]
        start = jnp.minimum(low, blocks - reach)
        block = offset + start
        bias = jnp.where((block >= low) & (block < high), 0.0, NEG)
        k = k_ref[pl.ds(start, reach), k_at].reshape(width, HD)
        v = gen(pl.ds(start, reach)).reshape(width, HD)
        out = attend(q_ref[pl.ds(i, 1), q_at], k, v, bias)
        score = (out[0] - gen(i).astype(jnp.float32)).astype(jnp.bfloat16)
        if o_at is None:
            o_ref[1] = score
        else:
            o_ref[i, o_at] = score


def cost(heads, blocks, units):
    return pl.CostEstimate(
        flops=heads * blocks * blocks * 4 * TOK * TOK * HD,
        bytes_accessed=units * blocks * TOK * HD * 2,
        transcendentals=heads * blocks * blocks * TOK * TOK,
    )


def pack(plan, ranges, tensors):
    peers, units = len(plan), len(plan[0])
    widths = [count * HD for _, count in ranges]
    starts = [sum(widths[:r]) for r in range(len(ranges))]

    def place(h):
        for r, (head, count) in enumerate(ranges):
            if head <= h < head + count:
                return r, starts[r] + (h - head) * HD

    need = []
    for u in range(units):
        need.append(list(dict.fromkeys((plan[p][u][0], place(plan[p][u][1])[0]) for p in range(peers))))
    order = sorted(range(units), key=lambda u: (len(need[u]), u))
    fetch = list(dict.fromkeys(piece for u in order for piece in need[u]))

    def body(*refs):
        o_ref, rows, tiles, in_sem, out_sem = refs[len(tensors) :]
        copies = {}
        for n, (t, r) in enumerate(fetch):
            source = refs[t].at[0, :, pl.ds(ranges[r][0] * HD, widths[r])]
            target = rows.at[t, :, pl.ds(starts[r], widths[r])]
            copies[t, r] = pltpu.make_async_copy(source, target, in_sem.at[n])
            copies[t, r].start()
        sent = []
        for u in order:
            for piece in need[u]:
                if piece in copies:
                    copies.pop(piece).wait()
            for p in range(peers):
                t, h = plan[p][u]
                at = place(h)[1]
                tiles[p, u] = rows[t, :, at : at + HD]
            sent.append(pltpu.make_async_copy(tiles.at[:, u], o_ref.at[:, u], out_sem.at[u]))
            sent[-1].start()
        for copy in sent:
            copy.wait()

    return pl.pallas_call(
        body,
        in_specs=[pl.BlockSpec(memory_space=pl.ANY)] * len(tensors),
        out_specs=pl.BlockSpec(memory_space=pl.ANY),
        out_shape=jax.ShapeDtypeStruct((peers, units, TOK, HD), jnp.bfloat16),
        scratch_shapes=[
            pltpu.VMEM((len(tensors), TOK, sum(widths)), jnp.bfloat16),
            pltpu.VMEM((peers, units, TOK, HD), jnp.bfloat16),
            pltpu.SemaphoreType.DMA((len(fetch),)),
            pltpu.SemaphoreType.DMA((units,)),
        ],
        compiler_params=WHOLE,
        cost_estimate=cost(0, peers, 2 * units),
    )(*tensors)


def unpack(places, back):
    def body(x_ref, *o_refs):
        for o_ref, place in zip(o_refs, places):
            for h, (p, u) in enumerate(place):
                o_ref[0, :, h * HD : (h + 1) * HD] = x_ref[p, u]

    width = len(places[0]) * HD
    return pl.pallas_call(
        body,
        out_shape=[jax.ShapeDtypeStruct((1, TOK, width), jnp.bfloat16) for _ in places],
        compiler_params=LOCAL,
        cost_estimate=cost(0, 1, 4 * len(places[0])),
    )(back)


def student_kernel(blocks, first, role, arrived):
    def body(first_ref, role_ref, x_ref, o_ref):
        @pl.when(role_ref[0] == 1)
        def _():
            sources = [(x_ref, t) for t in range(3)]
            student_head(range(0, blocks, 2), first_ref[0], sources, o_ref, 0)

    return pl.pallas_call(
        body,
        in_specs=[SMEM, SMEM, VMEM],
        out_specs=VMEM,
        out_shape=jax.ShapeDtypeStruct((blocks, 1, TOK, HD), jnp.bfloat16),
        compiler_params=LOCAL,
        cost_estimate=cost(1, blocks, 4),
    )(first, role, arrived)


def rest_teacher(blocks, clips, role, arrived, offset, gen, shared):
    def body(clip_ref, role_ref, x_ref, gen_ref, shared_ref, o_ref):
        @pl.when(role_ref[0] == 1)
        def _():
            o_ref[...] = gen_ref[...]

        @pl.when(role_ref[0] == 2)
        def _():
            sources = [(x_ref, offset + t) for t in range(2)]
            teacher_head(
                blocks, range(blocks), clip_ref, sources, lambda at: shared_ref[at, 0], o_ref, 0
            )

    return pl.pallas_call(
        body,
        in_specs=[SMEM, SMEM, VMEM, VMEM, VMEM],
        out_specs=VMEM,
        out_shape=jax.ShapeDtypeStruct((blocks, 1, TOK, HD), jnp.bfloat16),
        compiler_params=LOCAL,
        cost_estimate=cost(1, blocks, 5),
    )(clips, role, arrived, gen, shared)


def slots_kernel(full, blocks, first, clips, arrived):
    def body(first_ref, clip_ref, x_ref, o_ref):
        def head(s, carry):
            sources = [(x_ref, 5 * s + t) for t in range(5)]
            student_head(range(0, blocks, 2), first_ref[0], sources[:3], o_ref, 2 * s)
            gen = lambda at: o_ref[at, 2 * s]
            teacher_head(blocks, range(blocks), clip_ref, sources[3:], gen, o_ref, 2 * s + 1)

        lax.fori_loop(0, full, head, None)

    return pl.pallas_call(
        body,
        in_specs=[SMEM, SMEM, VMEM],
        out_specs=VMEM,
        out_shape=jax.ShapeDtypeStruct((blocks, 2 * full, TOK, HD), jnp.bfloat16),
        compiler_params=LOCAL,
        cost_estimate=cost(2 * full, blocks, 7 * full),
    )(first, clips, arrived)


def rest_pack(base, columns, column, tensors):
    def body(column_ref, *refs):
        rows, sems = refs[-2:]
        copies = []
        for t in range(5):
            source = refs[t].at[0, :, pl.ds(base * HD, columns * HD)]
            copies.append(pltpu.make_async_copy(source, rows.at[t], sems.at[t]))
            copies[-1].start()
        for t in range(5):
            copies[t].wait()
            for s in range(columns):
                at = pl.multiple_of((column_ref[0] ^ s) * HD, HD)
                refs[5 + s][t] = rows[t, :, pl.ds(at, HD)]

    return pl.pallas_call(
        body,
        in_specs=[SMEM] + [pl.BlockSpec(memory_space=pl.ANY)] * 5,
        out_specs=[VMEM] * columns,
        out_shape=[jax.ShapeDtypeStruct((5, TOK, HD), jnp.bfloat16)] * columns,
        scratch_shapes=[
            pltpu.VMEM((5, TOK, columns * HD), jnp.bfloat16),
            pltpu.SemaphoreType.DMA((5,)),
        ],
        compiler_params=WHOLE,
        cost_estimate=cost(0, 1, 10 * columns),
    )(column, *tensors)


def rest_kernel(columns, first, clips, where, own, other):
    blocks = 2 * columns

    def body(first_ref, clip_ref, where_ref, *refs):
        x, gen = refs[-2:]
        column, side = where_ref[0], where_ref[1]
        mine = [2 * (column ^ s) + side for s in range(columns)]
        for s in range(columns):
            x[mine[s]] = refs[s][...]
            x[mine[s] ^ 1] = refs[columns + s][...]
        sources = [(x, t) for t in range(5)]
        student_head(range(0, blocks, 2), first_ref[0], sources[:3], gen, 0)
        at_gen = lambda at: gen[at, 0]
        for s in range(columns):
            o_ref = refs[2 * columns + s]
            o_ref[0:1] = gen[mine[s]]
            teacher_head(blocks, [mine[s]], clip_ref, sources[3:], at_gen, o_ref, None)

    return pl.pallas_call(
        body,
        in_specs=[SMEM] * 3 + [VMEM] * (2 * columns),
        out_specs=[VMEM] * columns,
        out_shape=[jax.ShapeDtypeStruct((2, TOK, HD), jnp.bfloat16)] * columns,
        scratch_shapes=[
            pltpu.VMEM((blocks, 5, TOK, HD), jnp.bfloat16),
            pltpu.VMEM((blocks, 1, TOK, HD), jnp.bfloat16),
        ],
        compiler_params=LOCAL,
        cost_estimate=cost(2, blocks, 7),
    )(first, clips, where, *own, *other)


def join(base, columns, places, column, back, pieces):
    def body(column_ref, x_ref, *refs):
        for i, o_ref in enumerate(refs[columns:]):
            for h, (p, u) in enumerate(places[i]):
                o_ref[0, :, h * HD : (h + 1) * HD] = x_ref[p, u]
            for s in range(columns):
                at = pl.multiple_of((base + (column_ref[0] ^ s)) * HD, HD)
                o_ref[0, :, pl.ds(at, HD)] = refs[s][i]

    width = (base + columns) * HD
    return pl.pallas_call(
        body,
        in_specs=[SMEM, VMEM] + [VMEM] * columns,
        out_specs=[VMEM] * 2,
        out_shape=[jax.ShapeDtypeStruct((1, TOK, width), jnp.bfloat16)] * 2,
        compiler_params=LOCAL,
        cost_estimate=cost(0, 1, 4 * (base + columns)),
    )(column, back, *pieces)


def by_slots_and_columns(tensors, peers, full, rest, first, clips):
    base = full * peers
    here = lax.axis_index("tm")
    column, side = here // 2, here % 2
    where = jnp.stack([column, side]).astype(jnp.int32)

    def swapped(x, by):
        return lax.ppermute(x, "tm", [(i, i ^ by) for i in range(peers)])

    plan = [[(t, s * peers + p) for s in range(full) for t in range(5)] for p in range(peers)]
    slots = [(s * peers, peers) for s in range(full)]
    arrived = lax.all_to_all(pack(plan, slots, tensors), "tm", 0, 0)
    pieces = rest_pack(base, rest, where[:1], tensors)
    near, far = pieces[:2], pieces[2:]
    arrived, far = lax.optimization_barrier((arrived, far))
    own = [pieces[0]] + [swapped(x, 2 * s) for s, x in enumerate(near) if s]
    own += [swapped(x, 2 * (s + len(near))) for s, x in enumerate(far)]
    other = [swapped(x, 1) for x in own]
    results = slots_kernel(full, peers, first, clips, arrived)
    back = lax.all_to_all(results, "tm", 0, 0)
    _, own, other = lax.optimization_barrier((results, own, other))
    pieces = rest_kernel(rest, first, clips, where, own, other)
    pieces = [swapped(x, 2 * s) if s else x for s, x in enumerate(pieces)]
    places = [[(h % peers, 2 * (h // peers) + i) for h in range(base)] for i in (0, 1)]
    return tuple(join(base, rest, places, where[:1], back, pieces))


def by_roles(tensors, peers, heads, first, clips):
    here = lax.axis_index("tm")
    role = jnp.where(here < 2 * heads, 1 + here % 2, 0).astype(jnp.int32)[None]
    plan = [
        [(t, min(p // 2, heads - 1)) for t in ((3, 4, 4) if p % 2 else (0, 1, 2))]
        for p in range(peers)
    ]
    arrived = lax.all_to_all(pack(plan, [(0, heads)], tensors), "tm", 0, 0)
    gen = student_kernel(peers, first, role, arrived)
    shared = lax.ppermute(gen, "tm", [(2 * r, 2 * r + 1) for r in range(heads)])
    results = rest_teacher(peers, clips, role, arrived, 0, gen, shared)
    back = lax.all_to_all(results, "tm", 0, 0)
    return tuple(unpack([[(2 * r + i, 0) for r in range(heads)] for i in (0, 1)], back))


def per_device(student_q, student_k, student_v, teacher_q, teacher_k, stagger, clip_lengths):
    heads = student_q.shape[2] // HD
    peers = lax.axis_size("tm")
    full, rest = divmod(heads, peers)
    running = jnp.cumsum(clip_lengths[0])
    block = jnp.arange(peers, dtype=jnp.int32)
    before = running[None, :] <= block[:, None]
    low = jnp.max(jnp.where(before, running[None, :], 0), axis=1)
    high = jnp.min(jnp.where(before, peers, running[None, :]), axis=1)
    clips = jnp.stack([low, high]).astype(jnp.int32)
    tensors = (student_q, student_k, student_v, teacher_q, teacher_k)
    if full == 0:
        assert 2 * rest <= peers
        return by_roles(tensors, peers, rest, stagger, clips)
    assert peers == 2 * rest and rest & (rest - 1) == 0
    return by_slots_and_columns(tensors, peers, full, rest, stagger, clips)


def solution(mesh):
    spec = P("seq", "tm", "mp")
    return jax.shard_map(
        per_device,
        mesh=mesh,
        in_specs=(spec,) * 5 + (P("seq"), P("seq", None)),
        out_specs=(spec, spec),
        check_vma=False,
    )
```

profile of v0, /device:TPU:0, one launch (start us, length us, event | category | flops | bytes accessed | tf_op | source)
XLA Modules:
  0.0 142.8 jit_solution(13319906411023903290)
XLA Ops:
  0.6 2.7 %shard_map.86 = bf16[8,10,128,128]{3,2,1,0:T(8,128)(2,1)} custom-call(bf16[1,128,2560]{2,1,0:T(8,128)(2,1)} %refs_0_.3, bf16[1,128,2560]{2,1,0:T(8,128)(2,1)} %refs_1_.3, bf16[1,128,2560]{2,1,0:T(8,128)(2,1)} %refs_2_.3, bf16[1,128,2560]{2,1,0:T(8,128)(2,1)} %refs_3_.3, bf16[1,128,2560]{2,1,0:T(8,128)(2,1)} %refs_4_.3), custom_call_target="tpu_custom_call" | custom-call | bytes 5242880 | tf_op jit(solution)/shard_map/pallas_call | solution.py:115
  3.4 0.0 copy-start.5
  3.4 7.3 %all-to-all-start = ((bf16[8,10,128,128]{3,2,1,0:T(8,128)(2,1)}), bf16[8,10,128,128]{3,2,1,0:T(8,128)(2,1)S(1)}, u32[]{:S(2)}, u32[]{:S(2)}) async-start(bf16[8,10,128,128]{3,2,1,0:T(8,128)(2,1)} %shard_map.86), calls=%async_computation | async-start | bytes 5242880 | tf_op jit(solution)/shard_map/all_to_all | solution.py:297
  11.3 0.0 copy-done.5
  11.3 0.2 reduce-window.8
  11.5 2.1 %shard_map.87 = (bf16[5,128,128]{2,1,0:T(8,128)(2,1)}, bf16[5,128,128]{2,1,0:T(8,128)(2,1)}, bf16[5,128,128]{2,1,0:T(8,128)(2,1)}, bf16[5,128,128]{2,1,0:T(8,128)(2,1)}) custom-call(s32[1]{0:T(128)} %bitcast.column_ref, bf16[1,128,2560]{2,1,0:T(8,128)(2,1)} %refs_0_.3, bf16[1,128,2560]{2,1,0:T(8,128)(2,1)} %refs_1_.3, bf16[1,128,2560]{2,1,0:T(8,128)(2,1)} %refs_2_.3, ...), custom_call_target="tpu_custom_call" | custom-call | bytes 1310720 | tf_op jit(solution)/shard_map/pallas_call | solution.py:220
  13.5 0.1 select_reduce_fusion.1
  13.6 56.5 %all-to-all-done.x_ref = bf16[8,10,128,128]{3,2,1,0:T(8,128)(2,1)S(1)} async-done(((bf16[8,10,128,128]{3,2,1,0:T(8,128)(2,1)}), bf16[8,10,128,128]{3,2,1,0:T(8,128)(2,1)S(1)}, u32[]{:S(2)}, u32[]{:S(2)}) %all-to-all-start) | async-done | bytes 2621472 | tf_op jit(solution)/shard_map/all_to_all | solution.py:297
  70.1 0.0 copy-start.4
  70.1 0.0 copy-start.3
  70.1 0.0 copy-start.2
  70.1 0.0 copy-start.1
  70.1 8.8 %shard_map.88 = bf16[8,4,128,128]{3,2,1,0:T(8,128)(2,1)S(1)} custom-call(s32[1]{0:T(128)S(6)} %copy.9.first_ref, s32[2,8]{1,0:T(2,128)S(1)} %pad_add_fusion.clip_ref, bf16[8,10,128,128]{3,2,1,0:T(8,128)(2,1)S(1)} %all-to-all-done.x_ref), custom_call_target="tpu_custom_call" | custom-call | flops 2147483648 | bytes 3670016 | tf_op jit(solution)/shard_map/pallas_call | solution.py:196
  78.9 0.0 copy-start
  78.9 1.0 copy-done
  79.9 3.6 %all-to-all-start.1 = ((bf16[8,4,128,128]{3,2,1,0:T(8,128)(2,1)}), bf16[8,4,128,128]{3,2,1,0:T(8,128)(2,1)S(1)}, u32[]{:S(2)}, u32[]{:S(2)}) async-start(bf16[8,4,128,128]{3,2,1,0:T(8,128)(2,1)} %copy-done), calls=%async_computation.1 | async-start | bytes 2097152 | tf_op jit(solution)/shard_map/all_to_all | solution.py:305
  83.5 0.0 copy-done.4
  83.5 2.0 %collective-permute-start = (bf16[5,128,128]{2,1,0:T(8,128)(2,1)S(1)}, bf16[5,128,128]{2,1,0:T(8,128)(2,1)S(1)}, u32[]{:S(2)}, u32[]{:S(2)}) collective-permute-start(bf16[5,128,128]{2,1,0:T(8,128)(2,1)S(1)} %copy-done.4), channel_id=1, source_target_pairs={{0,8},{4,12},{8,0},{12,4},{16,24},{20,28},{24,16},{28,20},{1,9},{5... | collective-permute-start | bytes 491528 | tf_op jit(solution)/shard_map/ppermute | solution.py:293
  85.5 0.0 copy-done.3
  85.5 2.4 %collective-permute-start.1 = (bf16[5,128,128]{2,1,0:T(8,128)(2,1)S(1)}, bf16[5,128,128]{2,1,0:T(8,128)(2,1)S(1)}, u32[]{:S(2)}, u32[]{:S(2)}) collective-permute-start(bf16[5,128,128]{2,1,0:T(8,128)(2,1)S(1)} %copy-done.3), channel_id=1, source_target_pairs={{0,16},{4,20},{8,24},{12,28},{16,0},{20,4},{24,8},{28,12},{1,17},{... | collective-permute-start | bytes 491528 | tf_op jit(solution)/shard_map/ppermute | solution.py:293
  87.9 0.0 copy-done.2
  87.9 0.1 collective-permute-start.2
  87.9 0.0 copy-done.1
  87.9 1.9 %collective-permute-start.3 = (bf16[5,128,128]{2,1,0:T(8,128)(2,1)S(1)}, bf16[5,128,128]{2,1,0:T(8,128)(2,1)S(1)}, u32[]{:S(2)}, u32[]{:S(2)}) collective-permute-start(bf16[5,128,128]{2,1,0:T(8,128)(2,1)S(1)} %copy-done.1), channel_id=1, source_target_pairs={{0,4},{4,0},{8,12},{12,8},{16,20},{20,16},{24,28},{28,24},{1,5},{5... | collective-permute-start | bytes 491528 | tf_op jit(solution)/shard_map/ppermute | solution.py:293
  89.9 15.8 %collective-permute-done.refs_1_ = bf16[5,128,128]{2,1,0:T(8,128)(2,1)S(1)} collective-permute-done((bf16[5,128,128]{2,1,0:T(8,128)(2,1)S(1)}, bf16[5,128,128]{2,1,0:T(8,128)(2,1)S(1)}, u32[]{:S(2)}, u32[]{:S(2)}) %collective-permute-start) | collective-permute-done | bytes 163872 | tf_op jit(solution)/shard_map/ppermute | solution.py:293
  105.7 1.5 %collective-permute-start.4 = (bf16[5,128,128]{2,1,0:T(8,128)(2,1)S(1)}, bf16[5,128,128]{2,1,0:T(8,128)(2,1)S(1)}, u32[]{:S(2)}, u32[]{:S(2)}) collective-permute-start(bf16[5,128,128]{2,1,0:T(8,128)(2,1)S(1)} %collective-permute-done.refs_1_), channel_id=1, source_target_pairs={{0,4},{4,0},{8,12},{12,8},{16,20},{20,16},{24,28},{28,24},{1,5},{5... | collective-permute-start | bytes 491528 | tf_op jit(solution)/shard_map/ppermute | solution.py:293
  107.2 13.9 %collective-permute-done.1.refs_2_ = bf16[5,128,128]{2,1,0:T(8,128)(2,1)S(1)} collective-permute-done((bf16[5,128,128]{2,1,0:T(8,128)(2,1)S(1)}, bf16[5,128,128]{2,1,0:T(8,128)(2,1)S(1)}, u32[]{:S(2)}, u32[]{:S(2)}) %collective-permute-start.1) | collective-permute-done | bytes 163872 | tf_op jit(solution)/shard_map/ppermute | solution.py:293
  121.2 1.3 collective-permute-start.5
  122.4 0.0 collective-permute-done.2.refs_3_
  122.4 0.8 collective-permute-start.6
  123.2 0.1 pad_add_fusion.1.where_ref
  123.3 0.0 collective-permute-done.3.refs_4_
  123.3 0.0 collective-permute-done.4.refs_5_
  123.3 3.5 %collective-permute-done.5.refs_6_ = bf16[5,128,128]{2,1,0:T(8,128)(2,1)S(1)} collective-permute-done((bf16[5,128,128]{2,1,0:T(8,128)(2,1)S(1)}, bf16[5,128,128]{2,1,0:T(8,128)(2,1)S(1)}, u32[]{:S(2)}, u32[]{:S(2)}) %collective-permute-start.5) | collective-permute-done | bytes 163872 | tf_op jit(solution)/shard_map/ppermute | solution.py:293
  126.8 1.8 %collective-permute-done.6.refs_7_ = bf16[5,128,128]{2,1,0:T(8,128)(2,1)S(1)} collective-permute-done((bf16[5,128,128]{2,1,0:T(8,128)(2,1)S(1)}, bf16[5,128,128]{2,1,0:T(8,128)(2,1)S(1)}, u32[]{:S(2)}, u32[]{:S(2)}) %collective-permute-start.6) | collective-permute-done | bytes 163872 | tf_op jit(solution)/shard_map/ppermute | solution.py:293
  128.5 3.6 %shard_map.89 = (bf16[2,128,128]{2,1,0:T(8,128)(2,1)S(1)}, bf16[2,128,128]{2,1,0:T(8,128)(2,1)S(1)}, bf16[2,128,128]{2,1,0:T(8,128)(2,1)S(1)}, bf16[2,128,128]{2,1,0:T(8,128)(2,1)S(1)}) custom-call(s32[1]{0:T(128)S(6)} %copy.9.first_ref, s32[2,8]{1,0:T(2,128)S(1)} %pad_add_fusion.clip_ref, s32[2]{0:T(128)S(1)} %pad_add_fusion.1.where_ref, ...), custom_call_target="tpu_custom_call" | custom-call | flops 1073741824 | bytes 1835008 | tf_op jit(solution)/shard_map/pallas_call | solution.py:252
  132.1 0.9 collective-permute-start.7
  133.0 2.4 %collective-permute-start.8 = (bf16[2,128,128]{2,1,0:T(8,128)(2,1)S(1)}, bf16[2,128,128]{2,1,0:T(8,128)(2,1)S(1)}, u32[]{:S(2)}, u32[]{:S(2)}) collective-permute-start(bf16[2,128,128]{2,1,0:T(8,128)(2,1)S(1)} %get-tuple-element.38), channel_id=1, source_target_pairs={{0,16},{4,20},{8,24},{12,28},{16,0},{20,4},{24,8},{28,12},{1,17},{... | collective-permute-start | bytes 196616 | tf_op jit(solution)/shard_map/ppermute | solution.py:293
  135.4 1.2 collective-permute-start.9
  136.6 0.0 collective-permute-done.7.refs_1_
  136.6 1.6 %collective-permute-done.8.refs_2_ = bf16[2,128,128]{2,1,0:T(8,128)(2,1)S(1)} collective-permute-done((bf16[2,128,128]{2,1,0:T(8,128)(2,1)S(1)}, bf16[2,128,128]{2,1,0:T(8,128)(2,1)S(1)}, u32[]{:S(2)}, u32[]{:S(2)}) %collective-permute-start.8) | collective-permute-done | bytes 65568 | tf_op jit(solution)/shard_map/ppermute | solution.py:293
  138.2 3.3 %collective-permute-done.9.refs_3_ = bf16[2,128,128]{2,1,0:T(8,128)(2,1)S(1)} collective-permute-done((bf16[2,128,128]{2,1,0:T(8,128)(2,1)S(1)}, bf16[2,128,128]{2,1,0:T(8,128)(2,1)S(1)}, u32[]{:S(2)}, u32[]{:S(2)}) %collective-permute-start.9) | collective-permute-done | bytes 65568 | tf_op jit(solution)/shard_map/ppermute | solution.py:293
  141.5 0.0 all-to-all-done.1.x_ref
  141.5 1.3 shard_map.90
  (1 shorter events, 0.0 us)
Async XLA Ops:
  3.4 7.9 %copy-start.5 = (s32[1,3]{1,0:T(1,128)S(1)}, s32[1,3]{1,0:T(1,128)}, u32[]{:S(2)}) copy-start(s32[1,3]{1,0:T(1,128)} %param.13) | copy-start | bytes 40
  3.4 66.7 %all-to-all-start = ((bf16[8,10,128,128]{3,2,1,0:T(8,128)(2,1)}), bf16[8,10,128,128]{3,2,1,0:T(8,128)(2,1)S(1)}, u32[]{:S(2)}, u32[]{:S(2)}) async-start(bf16[8,10,128,128]{3,2,1,0:T(8,128)(2,1)} %shard_map.86), calls=%async_computation | async-start | bytes 5242880 | tf_op jit(solution)/shard_map/all_to_all | solution.py:297
  70.1 13.4 %copy-start.4 = (bf16[5,128,128]{2,1,0:T(8,128)(2,1)S(1)}, bf16[5,128,128]{2,1,0:T(8,128)(2,1)}, u32[]{:S(2)}) copy-start(bf16[5,128,128]{2,1,0:T(8,128)(2,1)} %get-tuple-element.25) | copy-start | bytes 491524
  70.1 15.4 %copy-start.3 = (bf16[5,128,128]{2,1,0:T(8,128)(2,1)S(1)}, bf16[5,128,128]{2,1,0:T(8,128)(2,1)}, u32[]{:S(2)}) copy-start(bf16[5,128,128]{2,1,0:T(8,128)(2,1)} %get-tuple-element.26) | copy-start | bytes 491524
  70.1 17.8 %copy-start.2 = (bf16[5,128,128]{2,1,0:T(8,128)(2,1)S(1)}, bf16[5,128,128]{2,1,0:T(8,128)(2,1)}, u32[]{:S(2)}) copy-start(bf16[5,128,128]{2,1,0:T(8,128)(2,1)} %get-tuple-element.27) | copy-start | bytes 491524
  70.1 17.8 %copy-start.1 = (bf16[5,128,128]{2,1,0:T(8,128)(2,1)S(1)}, bf16[5,128,128]{2,1,0:T(8,128)(2,1)}, u32[]{:S(2)}) copy-start(bf16[5,128,128]{2,1,0:T(8,128)(2,1)} %get-tuple-element.28.refs_0_) | copy-start | bytes 491524
  78.9 1.0 copy-start
  79.9 61.6 %all-to-all-start.1 = ((bf16[8,4,128,128]{3,2,1,0:T(8,128)(2,1)}), bf16[8,4,128,128]{3,2,1,0:T(8,128)(2,1)S(1)}, u32[]{:S(2)}, u32[]{:S(2)}) async-start(bf16[8,4,128,128]{3,2,1,0:T(8,128)(2,1)} %copy-done), calls=%async_computation.1 | async-start | bytes 2097152 | tf_op jit(solution)/shard_map/all_to_all | solution.py:305
  83.5 22.2 %collective-permute-start = (bf16[5,128,128]{2,1,0:T(8,128)(2,1)S(1)}, bf16[5,128,128]{2,1,0:T(8,128)(2,1)S(1)}, u32[]{:S(2)}, u32[]{:S(2)}) collective-permute-start(bf16[5,128,128]{2,1,0:T(8,128)(2,1)S(1)} %copy-done.4), channel_id=1, source_target_pairs={{0,8},{4,12},{8,0},{12,4},{16,24},{20,28},{24,16},{28,20},{1,9},{5... | collective-permute-start | bytes 491528 | tf_op jit(solution)/shard_map/ppermute | solution.py:293
  85.5 35.7 %collective-permute-start.1 = (bf16[5,128,128]{2,1,0:T(8,128)(2,1)S(1)}, bf16[5,128,128]{2,1,0:T(8,128)(2,1)S(1)}, u32[]{:S(2)}, u32[]{:S(2)}) collective-permute-start(bf16[5,128,128]{2,1,0:T(8,128)(2,1)S(1)} %copy-done.3), channel_id=1, source_target_pairs={{0,16},{4,20},{8,24},{12,28},{16,0},{20,4},{24,8},{28,12},{1,17},{... | collective-permute-start | bytes 491528 | tf_op jit(solution)/shard_map/ppermute | solution.py:293
  87.9 34.6 %collective-permute-start.2 = (bf16[5,128,128]{2,1,0:T(8,128)(2,1)S(1)}, bf16[5,128,128]{2,1,0:T(8,128)(2,1)S(1)}, u32[]{:S(2)}, u32[]{:S(2)}) collective-permute-start(bf16[5,128,128]{2,1,0:T(8,128)(2,1)S(1)} %copy-done.2), channel_id=1, source_target_pairs={{0,24},{4,28},{8,16},{12,20},{16,8},{20,12},{24,0},{28,4},{1,25},{... | collective-permute-start | bytes 491528 | tf_op jit(solution)/shard_map/ppermute | solution.py:293
  87.9 35.3 %collective-permute-start.3 = (bf16[5,128,128]{2,1,0:T(8,128)(2,1)S(1)}, bf16[5,128,128]{2,1,0:T(8,128)(2,1)S(1)}, u32[]{:S(2)}, u32[]{:S(2)}) collective-permute-start(bf16[5,128,128]{2,1,0:T(8,128)(2,1)S(1)} %copy-done.1), channel_id=1, source_target_pairs={{0,4},{4,0},{8,12},{12,8},{16,20},{20,16},{24,28},{28,24},{1,5},{5... | collective-permute-start | bytes 491528 | tf_op jit(solution)/shard_map/ppermute | solution.py:293
  105.7 17.6 %collective-permute-start.4 = (bf16[5,128,128]{2,1,0:T(8,128)(2,1)S(1)}, bf16[5,128,128]{2,1,0:T(8,128)(2,1)S(1)}, u32[]{:S(2)}, u32[]{:S(2)}) collective-permute-start(bf16[5,128,128]{2,1,0:T(8,128)(2,1)S(1)} %collective-permute-done.refs_1_), channel_id=1, source_target_pairs={{0,4},{4,0},{8,12},{12,8},{16,20},{20,16},{24,28},{28,24},{1,5},{5... | collective-permute-start | bytes 491528 | tf_op jit(solution)/shard_map/ppermute | solution.py:293
  121.2 5.6 %collective-permute-start.5 = (bf16[5,128,128]{2,1,0:T(8,128)(2,1)S(1)}, bf16[5,128,128]{2,1,0:T(8,128)(2,1)S(1)}, u32[]{:S(2)}, u32[]{:S(2)}) collective-permute-start(bf16[5,128,128]{2,1,0:T(8,128)(2,1)S(1)} %collective-permute-done.1.refs_2_), channel_id=1, source_target_pairs={{0,4},{4,0},{8,12},{12,8},{16,20},{20,16},{24,28},{28,24},{1,5},{5... | collective-permute-start | bytes 491528 | tf_op jit(solution)/shard_map/ppermute | solution.py:293
  122.4 6.1 %collective-permute-start.6 = (bf16[5,128,128]{2,1,0:T(8,128)(2,1)S(1)}, bf16[5,128,128]{2,1,0:T(8,128)(2,1)S(1)}, u32[]{:S(2)}, u32[]{:S(2)}) collective-permute-start(bf16[5,128,128]{2,1,0:T(8,128)(2,1)S(1)} %collective-permute-done.2.refs_3_), channel_id=1, source_target_pairs={{0,4},{4,0},{8,12},{12,8},{16,20},{20,16},{24,28},{28,24},{1,5},{5... | collective-permute-start | bytes 491528 | tf_op jit(solution)/shard_map/ppermute | solution.py:293
  132.1 4.5 %collective-permute-start.7 = (bf16[2,128,128]{2,1,0:T(8,128)(2,1)S(1)}, bf16[2,128,128]{2,1,0:T(8,128)(2,1)S(1)}, u32[]{:S(2)}, u32[]{:S(2)}) collective-permute-start(bf16[2,128,128]{2,1,0:T(8,128)(2,1)S(1)} %get-tuple-element.37), channel_id=1, source_target_pairs={{0,8},{4,12},{8,0},{12,4},{16,24},{20,28},{24,16},{28,20},{1,9},{5... | collective-permute-start | bytes 196616 | tf_op jit(solution)/shard_map/ppermute | solution.py:293
  133.0 5.2 %collective-permute-start.8 = (bf16[2,128,128]{2,1,0:T(8,128)(2,1)S(1)}, bf16[2,128,128]{2,1,0:T(8,128)(2,1)S(1)}, u32[]{:S(2)}, u32[]{:S(2)}) collective-permute-start(bf16[2,128,128]{2,1,0:T(8,128)(2,1)S(1)} %get-tuple-element.38), channel_id=1, source_target_pairs={{0,16},{4,20},{8,24},{12,28},{16,0},{20,4},{24,8},{28,12},{1,17},{... | collective-permute-start | bytes 196616 | tf_op jit(solution)/shard_map/ppermute | solution.py:293
  135.4 6.1 %collective-permute-start.9 = (bf16[2,128,128]{2,1,0:T(8,128)(2,1)S(1)}, bf16[2,128,128]{2,1,0:T(8,128)(2,1)S(1)}, u32[]{:S(2)}, u32[]{:S(2)}) collective-permute-start(bf16[2,128,128]{2,1,0:T(8,128)(2,1)S(1)} %get-tuple-element.39), channel_id=1, source_target_pairs={{0,24},{4,28},{8,16},{12,20},{16,8},{20,12},{24,0},{28,4},{1,25},{... | collective-permute-start | bytes 196616 | tf_op jit(solution)/shard_map/ppermute | solution.py:293
where the time goes:
time: 143 us
  waiting for transfers between devices  96.4 us (67%)
  starting transfers between devices  25.3 us (18%)
  Pallas kernels  18.4 us (13%)
    all_to_all x1, waiting for transfers between devices, by_slots_and_columns(): arrived = lax.all_to_all(pack(plan, slots, tensors), 'tm', 0, 0)  56.5 us
    ppermute x10, waiting for transfers between devices, swapped(): return lax.ppermute(x, 'tm', [(i, i ^ by) for i in range(peers)])  39.9 us
    ppermute x10, starting transfers between devices, swapped(): return lax.ppermute(x, 'tm', [(i, i ^ by) for i in range(peers)])  14.4 us
    pallas_call x1, Pallas kernels, slots_kernel(): pl.pallas_call(body, in_specs=[SMEM, SMEM, VMEM], out_specs=VMEM, out_sha...  8.77 us
    all_to_all x1, starting transfers between devices, by_slots_and_columns(): arrived = lax.all_to_all(pack(plan, slots, tensors), 'tm', 0, 0)  7.26 us
    all_to_all x1, starting transfers between devices, by_slots_and_columns(): back = lax.all_to_all(results, 'tm', 0, 0)  3.6 us
    pallas_call x1, Pallas kernels, rest_kernel(): pl.pallas_call(body, in_specs=[SMEM] * 3 + [VMEM] * (2 * columns), out_sp...  3.58 us
  transfers between devices with their start and end apart: 12, of which 7 were waited for; matrix products, arithmetic and copies ran while one was open for 0% of the time, Pallas kernels for 4%

commit v1 on v0

--- a/solution.py
+++ b/solution.py
@@ -296,15 +296,12 @@
     slots = [(s * peers, peers) for s in range(full)]
     arrived = lax.all_to_all(pack(plan, slots, tensors), "tm", 0, 0)
     pieces = rest_pack(base, rest, where[:1], tensors)
-    near, far = pieces[:2], pieces[2:]
-    arrived, far = lax.optimization_barrier((arrived, far))
-    own = [pieces[0]] + [swapped(x, 2 * s) for s, x in enumerate(near) if s]
-    own += [swapped(x, 2 * (s + len(near))) for s, x in enumerate(far)]
+    own = [swapped(x, 2 * s) if s else x for s, x in enumerate(pieces)]
     other = [swapped(x, 1) for x in own]
+    pieces = rest_kernel(rest, first, clips, where, own, other)
+    arrived, _ = lax.optimization_barrier((arrived, pieces))
     results = slots_kernel(full, peers, first, clips, arrived)
     back = lax.all_to_all(results, "tm", 0, 0)
-    _, own, other = lax.optimization_barrier((results, own, other))
-    pieces = rest_kernel(rest, first, clips, where, own, other)
     pieces = [swapped(x, 2 * s) if s else x for s, x in enumerate(pieces)]
     places = [[(h % peers, 2 * (h // peers) + i) for h in range(base)] for i in (0, 1)]
     return tuple(join(base, rest, places, where[:1], back, pieces))

time: 143 us -> 140 us (0.979)
  waiting for transfers between devices: 96.4 us -> 91.1 us
    all_to_all x1, waiting for transfers between devices: 56.5 us -> 0.01 us  [by_slots_and_columns(): arrived = lax.all_to_all(pack(plan, slots, tensors), 'tm', 0, 0)]
    ppermute x10, waiting for transfers between devices: 39.9 us -> 91 us  [swapped(): return lax.ppermute(x, 'tm', [(i, i ^ by) for i in range(peers)])]
  transfers between devices with their start and end apart: 12 -> 12, of which waited for: 7 -> 6; matrix products, arithmetic and copies ran while one was open for 0% -> 0% of each run, Pallas kernels for 4% -> 4%
where the time goes in v1:
time: 140 us; the launch traced here: 139 us
  waiting for transfers between devices  91.1 us (65%)
  starting transfers between devices  26.5 us (19%)
  Pallas kernels  18.3 us (13%)
  local copies, waits for them, and re-layouts  1.88 us (1%)
    ppermute x10, waiting for transfers between devices, swapped(): return lax.ppermute(x, 'tm', [(i, i ^ by) for i in range(peers)])  91 us
    ppermute x10, starting transfers between devices, swapped(): return lax.ppermute(x, 'tm', [(i, i ^ by) for i in range(peers)])  14.5 us
    pallas_call x1, Pallas kernels, slots_kernel(): pl.pallas_call(body, in_specs=[SMEM, SMEM, VMEM], out_specs=VMEM, out_sha...  8.75 us
    all_to_all x1, starting transfers between devices, by_slots_and_columns(): arrived = lax.all_to_all(pack(plan, slots, tensors), 'tm', 0, 0)  7.26 us
    all_to_all x1, starting transfers between devices, by_slots_and_columns(): back = lax.all_to_all(results, 'tm', 0, 0)  4.77 us
    pallas_call x1, Pallas kernels, rest_kernel(): pl.pallas_call(body, in_specs=[SMEM] * 3 + [VMEM] * (2 * columns), out_sp...  3.58 us
  transfers between devices with their start and end apart: 12, of which 6 were waited for; matrix products, arithmetic and copies ran while one was open for 0% of the time, Pallas kernels for 4%

profile of v1, /device:TPU:0, one launch (start us, length us, event | category | flops | bytes accessed | tf_op | source)
XLA Modules:
  0.0 139.5 jit_solution(4012348030410140719)
XLA Ops:
  0.6 2.7 %shard_map.86 = bf16[8,10,128,128]{3,2,1,0:T(8,128)(2,1)} custom-call(bf16[1,128,2560]{2,1,0:T(8,128)(2,1)} %refs_0_.3, bf16[1,128,2560]{2,1,0:T(8,128)(2,1)} %refs_1_.3, bf16[1,128,2560]{2,1,0:T(8,128)(2,1)} %refs_2_.3, bf16[1,128,2560]{2,1,0:T(8,128)(2,1)} %refs_3_.3, bf16[1,128,2560]{2,1,0:T(8,128)(2,1)} %refs_4_.3), custom_call_target="tpu_custom_call" | custom-call | bytes 5242880 | tf_op jit(solution)/shard_map/pallas_call | solution.py:115
  3.3 7.3 %all-to-all-start = ((bf16[8,10,128,128]{3,2,1,0:T(8,128)(2,1)}), bf16[8,10,128,128]{3,2,1,0:T(8,128)(2,1)S(1)}, u32[]{:S(2)}, u32[]{:S(2)}) async-start(bf16[8,10,128,128]{3,2,1,0:T(8,128)(2,1)} %shard_map.86), calls=%async_computation | async-start | bytes 5242880 | tf_op jit(solution)/shard_map/all_to_all | solution.py:297
  10.6 0.0 copy-start.2
  10.6 2.1 %shard_map.87 = (bf16[5,128,128]{2,1,0:T(8,128)(2,1)}, bf16[5,128,128]{2,1,0:T(8,128)(2,1)}, bf16[5,128,128]{2,1,0:T(8,128)(2,1)}, bf16[5,128,128]{2,1,0:T(8,128)(2,1)}) custom-call(s32[1]{0:T(128)} %bitcast.column_ref, bf16[1,128,2560]{2,1,0:T(8,128)(2,1)} %refs_0_.3, bf16[1,128,2560]{2,1,0:T(8,128)(2,1)} %refs_1_.3, bf16[1,128,2560]{2,1,0:T(8,128)(2,1)} %refs_2_.3, ...), custom_call_target="tpu_custom_call" | custom-call | bytes 1310720 | tf_op jit(solution)/shard_map/pallas_call | solution.py:220
  12.7 2.1 %collective-permute-start = (bf16[5,128,128]{2,1,0:T(8,128)(2,1)}, bf16[5,128,128]{2,1,0:T(8,128)(2,1)S(1)}, u32[]{:S(2)}, u32[]{:S(2)}) collective-permute-start(bf16[5,128,128]{2,1,0:T(8,128)(2,1)} %get-tuple-element.12), channel_id=1, source_target_pairs={{0,8},{4,12},{8,0},{12,4},{16,24},{20,28},{24,16},{28,20},{1,9},{5... | collective-permute-start | bytes 491528 | tf_op jit(solution)/shard_map/ppermute | solution.py:293
  14.7 2.4 %collective-permute-start.1 = (bf16[5,128,128]{2,1,0:T(8,128)(2,1)}, bf16[5,128,128]{2,1,0:T(8,128)(2,1)S(1)}, u32[]{:S(2)}, u32[]{:S(2)}) collective-permute-start(bf16[5,128,128]{2,1,0:T(8,128)(2,1)} %get-tuple-element.13), channel_id=1, source_target_pairs={{0,16},{4,20},{8,24},{12,28},{16,0},{20,4},{24,8},{28,12},{1,17},{... | collective-permute-start | bytes 491528 | tf_op jit(solution)/shard_map/ppermute | solution.py:293
  17.1 0.1 collective-permute-start.2
  17.2 1.9 %collective-permute-start.3 = (bf16[5,128,128]{2,1,0:T(8,128)(2,1)}, bf16[5,128,128]{2,1,0:T(8,128)(2,1)S(1)}, u32[]{:S(2)}, u32[]{:S(2)}) collective-permute-start(bf16[5,128,128]{2,1,0:T(8,128)(2,1)} %get-tuple-element.11.refs_0_), channel_id=1, source_target_pairs={{0,4},{4,0},{8,12},{12,8},{16,20},{20,16},{24,28},{28,24},{1,5},{5... | collective-permute-start | bytes 491528 | tf_op jit(solution)/shard_map/ppermute | solution.py:293
  19.1 0.0 copy-done.2
  19.1 0.2 reduce-window.8
  19.3 0.1 select_reduce_fusion.1
  19.4 39.3 %collective-permute-done.refs_1_ = bf16[5,128,128]{2,1,0:T(8,128)(2,1)S(1)} collective-permute-done((bf16[5,128,128]{2,1,0:T(8,128)(2,1)}, bf16[5,128,128]{2,1,0:T(8,128)(2,1)S(1)}, u32[]{:S(2)}, u32[]{:S(2)}) %collective-permute-start) | collective-permute-done | bytes 163872 | tf_op jit(solution)/shard_map/ppermute | solution.py:293
  58.7 1.6 %collective-permute-start.4 = (bf16[5,128,128]{2,1,0:T(8,128)(2,1)S(1)}, bf16[5,128,128]{2,1,0:T(8,128)(2,1)S(1)}, u32[]{:S(2)}, u32[]{:S(2)}) collective-permute-start(bf16[5,128,128]{2,1,0:T(8,128)(2,1)S(1)} %collective-permute-done.refs_1_), channel_id=1, source_target_pairs={{0,4},{4,0},{8,12},{12,8},{16,20},{20,16},{24,28},{28,24},{1,5},{5... | collective-permute-start | bytes 491528 | tf_op jit(solution)/shard_map/ppermute | solution.py:293
  60.3 21.7 %collective-permute-done.1.refs_2_ = bf16[5,128,128]{2,1,0:T(8,128)(2,1)S(1)} collective-permute-done((bf16[5,128,128]{2,1,0:T(8,128)(2,1)}, bf16[5,128,128]{2,1,0:T(8,128)(2,1)S(1)}, u32[]{:S(2)}, u32[]{:S(2)}) %collective-permute-start.1) | collective-permute-done | bytes 163872 | tf_op jit(solution)/shard_map/ppermute | solution.py:293
  82.0 1.1 collective-permute-start.5
  83.1 0.0 collective-permute-done.2.refs_3_
  83.1 0.9 collective-permute-start.6
  84.0 0.1 pad_add_fusion.1.where_ref
  84.8 0.0 collective-permute-done.3.refs_4_
  84.8 0.0 collective-permute-done.4.refs_5_
  84.8 2.5 %collective-permute-done.5.refs_6_ = bf16[5,128,128]{2,1,0:T(8,128)(2,1)S(1)} collective-permute-done((bf16[5,128,128]{2,1,0:T(8,128)(2,1)S(1)}, bf16[5,128,128]{2,1,0:T(8,128)(2,1)S(1)}, u32[]{:S(2)}, u32[]{:S(2)}) %collective-permute-start.5) | collective-permute-done | bytes 163872 | tf_op jit(solution)/shard_map/ppermute | solution.py:293
  87.3 1.8 %collective-permute-done.6.refs_7_ = bf16[5,128,128]{2,1,0:T(8,128)(2,1)S(1)} collective-permute-done((bf16[5,128,128]{2,1,0:T(8,128)(2,1)S(1)}, bf16[5,128,128]{2,1,0:T(8,128)(2,1)S(1)}, u32[]{:S(2)}, u32[]{:S(2)}) %collective-permute-start.6) | collective-permute-done | bytes 163872 | tf_op jit(solution)/shard_map/ppermute | solution.py:293
  89.1 0.0 copy-start.1
  89.1 0.9 copy-done.1
  90.0 3.6 %shard_map.88 = (bf16[2,128,128]{2,1,0:T(8,128)(2,1)S(1)}, bf16[2,128,128]{2,1,0:T(8,128)(2,1)S(1)}, bf16[2,128,128]{2,1,0:T(8,128)(2,1)S(1)}, bf16[2,128,128]{2,1,0:T(8,128)(2,1)S(1)}) custom-call(s32[1]{0:T(128)S(6)} %copy.9.first_ref, s32[2,8]{1,0:T(2,128)S(1)} %pad_add_fusion.clip_ref, s32[2]{0:T(128)S(1)} %pad_add_fusion.1.where_ref, ...), custom_call_target="tpu_custom_call" | custom-call | flops 1073741824 | bytes 1835008 | tf_op jit(solution)/shard_map/pallas_call | solution.py:252
  93.6 0.0 all-to-all-done.x_ref
  93.6 8.8 %shard_map.89 = bf16[8,4,128,128]{3,2,1,0:T(8,128)(2,1)S(1)} custom-call(s32[1]{0:T(128)S(6)} %copy.9.first_ref, s32[2,8]{1,0:T(2,128)S(1)} %pad_add_fusion.clip_ref, bf16[8,10,128,128]{3,2,1,0:T(8,128)(2,1)S(1)} %all-to-all-done.x_ref), custom_call_target="tpu_custom_call" | custom-call | flops 2147483648 | bytes 3670016 | tf_op jit(solution)/shard_map/pallas_call | solution.py:196
  102.3 0.0 copy-start
  102.3 1.0 copy-done
  103.3 4.8 %all-to-all-start.1 = ((bf16[8,4,128,128]{3,2,1,0:T(8,128)(2,1)}), bf16[8,4,128,128]{3,2,1,0:T(8,128)(2,1)S(1)}, u32[]{:S(2)}, u32[]{:S(2)}) async-start(bf16[8,4,128,128]{3,2,1,0:T(8,128)(2,1)} %copy-done), calls=%async_computation.1 | async-start | bytes 2097152 | tf_op jit(solution)/shard_map/all_to_all | solution.py:304
  108.1 2.0 %collective-permute-start.7 = (bf16[2,128,128]{2,1,0:T(8,128)(2,1)S(1)}, bf16[2,128,128]{2,1,0:T(8,128)(2,1)S(1)}, u32[]{:S(2)}, u32[]{:S(2)}) collective-permute-start(bf16[2,128,128]{2,1,0:T(8,128)(2,1)S(1)} %get-tuple-element.16), channel_id=1, source_target_pairs={{0,8},{4,12},{8,0},{12,4},{16,24},{20,28},{24,16},{28,20},{1,9},{5... | collective-permute-start | bytes 196616 | tf_op jit(solution)/shard_map/ppermute | solution.py:293
  110.1 2.4 %collective-permute-start.8 = (bf16[2,128,128]{2,1,0:T(8,128)(2,1)S(1)}, bf16[2,128,128]{2,1,0:T(8,128)(2,1)S(1)}, u32[]{:S(2)}, u32[]{:S(2)}) collective-permute-start(bf16[2,128,128]{2,1,0:T(8,128)(2,1)S(1)} %get-tuple-element.17), channel_id=1, source_target_pairs={{0,16},{4,20},{8,24},{12,28},{16,0},{20,4},{24,8},{28,12},{1,17},{... | collective-permute-start | bytes 196616 | tf_op jit(solution)/shard_map/ppermute | solution.py:293
  112.5 0.0 collective-permute-start.9
  112.5 14.7 %collective-permute-done.7.refs_1_ = bf16[2,128,128]{2,1,0:T(8,128)(2,1)S(1)} collective-permute-done((bf16[2,128,128]{2,1,0:T(8,128)(2,1)S(1)}, bf16[2,128,128]{2,1,0:T(8,128)(2,1)S(1)}, u32[]{:S(2)}, u32[]{:S(2)}) %collective-permute-start.7) | collective-permute-done | bytes 65568 | tf_op jit(solution)/shard_map/ppermute | solution.py:293
  127.2 11.0 %collective-permute-done.8.refs_2_ = bf16[2,128,128]{2,1,0:T(8,128)(2,1)S(1)} collective-permute-done((bf16[2,128,128]{2,1,0:T(8,128)(2,1)S(1)}, bf16[2,128,128]{2,1,0:T(8,128)(2,1)S(1)}, u32[]{:S(2)}, u32[]{:S(2)}) %collective-permute-start.8) | collective-permute-done | bytes 65568 | tf_op jit(solution)/shard_map/ppermute | solution.py:293
  138.2 0.0 collective-permute-done.9.refs_3_
  138.2 0.0 all-to-all-done.1.x_ref
  138.2 1.3 shard_map.90
  (1 shorter events, 0.0 us)
Async XLA Ops:
  3.3 90.3 %all-to-all-start = ((bf16[8,10,128,128]{3,2,1,0:T(8,128)(2,1)}), bf16[8,10,128,128]{3,2,1,0:T(8,128)(2,1)S(1)}, u32[]{:S(2)}, u32[]{:S(2)}) async-start(bf16[8,10,128,128]{3,2,1,0:T(8,128)(2,1)} %shard_map.86), calls=%async_computation | async-start | bytes 5242880 | tf_op jit(solution)/shard_map/all_to_all | solution.py:297
  10.6 8.6 %copy-start.2 = (s32[1,3]{1,0:T(1,128)S(1)}, s32[1,3]{1,0:T(1,128)}, u32[]{:S(2)}) copy-start(s32[1,3]{1,0:T(1,128)} %param.13) | copy-start | bytes 40
  12.7 46.1 %collective-permute-start = (bf16[5,128,128]{2,1,0:T(8,128)(2,1)}, bf16[5,128,128]{2,1,0:T(8,128)(2,1)S(1)}, u32[]{:S(2)}, u32[]{:S(2)}) collective-permute-start(bf16[5,128,128]{2,1,0:T(8,128)(2,1)} %get-tuple-element.12), channel_id=1, source_target_pairs={{0,8},{4,12},{8,0},{12,4},{16,24},{20,28},{24,16},{28,20},{1,9},{5... | collective-permute-start | bytes 491528 | tf_op jit(solution)/shard_map/ppermute | solution.py:293
  14.7 67.3 %collective-permute-start.1 = (bf16[5,128,128]{2,1,0:T(8,128)(2,1)}, bf16[5,128,128]{2,1,0:T(8,128)(2,1)S(1)}, u32[]{:S(2)}, u32[]{:S(2)}) collective-permute-start(bf16[5,128,128]{2,1,0:T(8,128)(2,1)} %get-tuple-element.13), channel_id=1, source_target_pairs={{0,16},{4,20},{8,24},{12,28},{16,0},{20,4},{24,8},{28,12},{1,17},{... | collective-permute-start | bytes 491528 | tf_op jit(solution)/shard_map/ppermute | solution.py:293
  17.1 66.0 %collective-permute-start.2 = (bf16[5,128,128]{2,1,0:T(8,128)(2,1)}, bf16[5,128,128]{2,1,0:T(8,128)(2,1)S(1)}, u32[]{:S(2)}, u32[]{:S(2)}) collective-permute-start(bf16[5,128,128]{2,1,0:T(8,128)(2,1)} %get-tuple-element.14), channel_id=1, source_target_pairs={{0,24},{4,28},{8,16},{12,20},{16,8},{20,12},{24,0},{28,4},{1,25},{... | collective-permute-start | bytes 491528 | tf_op jit(solution)/shard_map/ppermute | solution.py:293
  17.2 67.6 %collective-permute-start.3 = (bf16[5,128,128]{2,1,0:T(8,128)(2,1)}, bf16[5,128,128]{2,1,0:T(8,128)(2,1)S(1)}, u32[]{:S(2)}, u32[]{:S(2)}) collective-permute-start(bf16[5,128,128]{2,1,0:T(8,128)(2,1)} %get-tuple-element.11.refs_0_), channel_id=1, source_target_pairs={{0,4},{4,0},{8,12},{12,8},{16,20},{20,16},{24,28},{28,24},{1,5},{5... | collective-permute-start | bytes 491528 | tf_op jit(solution)/shard_map/ppermute | solution.py:293
  58.7 26.1 %collective-permute-start.4 = (bf16[5,128,128]{2,1,0:T(8,128)(2,1)S(1)}, bf16[5,128,128]{2,1,0:T(8,128)(2,1)S(1)}, u32[]{:S(2)}, u32[]{:S(2)}) collective-permute-start(bf16[5,128,128]{2,1,0:T(8,128)(2,1)S(1)} %collective-permute-done.refs_1_), channel_id=1, source_target_pairs={{0,4},{4,0},{8,12},{12,8},{16,20},{20,16},{24,28},{28,24},{1,5},{5... | collective-permute-start | bytes 491528 | tf_op jit(solution)/shard_map/ppermute | solution.py:293
  82.0 5.3 %collective-permute-start.5 = (bf16[5,128,128]{2,1,0:T(8,128)(2,1)S(1)}, bf16[5,128,128]{2,1,0:T(8,128)(2,1)S(1)}, u32[]{:S(2)}, u32[]{:S(2)}) collective-permute-start(bf16[5,128,128]{2,1,0:T(8,128)(2,1)S(1)} %collective-permute-done.1.refs_2_), channel_id=1, source_target_pairs={{0,4},{4,0},{8,12},{12,8},{16,20},{20,16},{24,28},{28,24},{1,5},{5... | collective-permute-start | bytes 491528 | tf_op jit(solution)/shard_map/ppermute | solution.py:293
  83.1 6.0 %collective-permute-start.6 = (bf16[5,128,128]{2,1,0:T(8,128)(2,1)S(1)}, bf16[5,128,128]{2,1,0:T(8,128)(2,1)S(1)}, u32[]{:S(2)}, u32[]{:S(2)}) collective-permute-start(bf16[5,128,128]{2,1,0:T(8,128)(2,1)S(1)} %collective-permute-done.2.refs_3_), channel_id=1, source_target_pairs={{0,4},{4,0},{8,12},{12,8},{16,20},{20,16},{24,28},{28,24},{1,5},{5... | collective-permute-start | bytes 491528 | tf_op jit(solution)/shard_map/ppermute | solution.py:293
  89.1 0.9 copy-start.1
  102.3 1.0 copy-start
  103.3 34.9 %all-to-all-start.1 = ((bf16[8,4,128,128]{3,2,1,0:T(8,128)(2,1)}), bf16[8,4,128,128]{3,2,1,0:T(8,128)(2,1)S(1)}, u32[]{:S(2)}, u32[]{:S(2)}) async-start(bf16[8,4,128,128]{3,2,1,0:T(8,128)(2,1)} %copy-done), calls=%async_computation.1 | async-start | bytes 2097152 | tf_op jit(solution)/shard_map/all_to_all | solution.py:304
  108.1 19.1 %collective-permute-start.7 = (bf16[2,128,128]{2,1,0:T(8,128)(2,1)S(1)}, bf16[2,128,128]{2,1,0:T(8,128)(2,1)S(1)}, u32[]{:S(2)}, u32[]{:S(2)}) collective-permute-start(bf16[2,128,128]{2,1,0:T(8,128)(2,1)S(1)} %get-tuple-element.16), channel_id=1, source_target_pairs={{0,8},{4,12},{8,0},{12,4},{16,24},{20,28},{24,16},{28,20},{1,9},{5... | collective-permute-start | bytes 196616 | tf_op jit(solution)/shard_map/ppermute | solution.py:293
  110.1 28.1 %collective-permute-start.8 = (bf16[2,128,128]{2,1,0:T(8,128)(2,1)S(1)}, bf16[2,128,128]{2,1,0:T(8,128)(2,1)S(1)}, u32[]{:S(2)}, u32[]{:S(2)}) collective-permute-start(bf16[2,128,128]{2,1,0:T(8,128)(2,1)S(1)} %get-tuple-element.17), channel_id=1, source_target_pairs={{0,16},{4,20},{8,24},{12,28},{16,0},{20,4},{24,8},{28,12},{1,17},{... | collective-permute-start | bytes 196616 | tf_op jit(solution)/shard_map/ppermute | solution.py:293
  112.5 25.7 %collective-permute-start.9 = (bf16[2,128,128]{2,1,0:T(8,128)(2,1)S(1)}, bf16[2,128,128]{2,1,0:T(8,128)(2,1)S(1)}, u32[]{:S(2)}, u32[]{:S(2)}) collective-permute-start(bf16[2,128,128]{2,1,0:T(8,128)(2,1)S(1)} %get-tuple-element.18), channel_id=1, source_target_pairs={{0,24},{4,28},{8,16},{12,20},{16,8},{20,12},{24,0},{28,4},{1,25},{... | collective-permute-start | bytes 196616 | tf_op jit(solution)/shard_map/ppermute | solution.py:293

commit v2 on v1

--- a/solution.py
+++ b/solution.py
@@ -60,10 +60,7 @@
         v = gen(pl.ds(start, reach)).reshape(width, HD)
         out = attend(q_ref[pl.ds(i, 1), q_at], k, v, bias)
         score = (out[0] - gen(i).astype(jnp.float32)).astype(jnp.bfloat16)
-        if o_at is None:
-            o_ref[1] = score
-        else:
-            o_ref[i, o_at] = score
+        o_ref[i, o_at] = score
 
 
 def cost(heads, blocks, units):
@@ -231,80 +228,81 @@
     )(column, *tensors)
 
 
-def rest_kernel(columns, first, clips, where, own, other):
-    blocks = 2 * columns
-
+def rest_kernel(blocks, first, clips, where, arrived):
     def body(first_ref, clip_ref, where_ref, *refs):
-        x, gen = refs[-2:]
-        column, side = where_ref[0], where_ref[1]
-        mine = [2 * (column ^ s) + side for s in range(columns)]
-        for s in range(columns):
-            x[mine[s]] = refs[s][...]
-            x[mine[s] ^ 1] = refs[columns + s][...]
-        sources = [(x, t) for t in range(5)]
-        student_head(range(0, blocks, 2), first_ref[0], sources[:3], gen, 0)
-        at_gen = lambda at: gen[at, 0]
-        for s in range(columns):
-            o_ref = refs[2 * columns + s]
-            o_ref[0:1] = gen[mine[s]]
-            teacher_head(blocks, [mine[s]], clip_ref, sources[3:], at_gen, o_ref, None)
-
-    return pl.pallas_call(
-        body,
-        in_specs=[SMEM] * 3 + [VMEM] * (2 * columns),
-        out_specs=[VMEM] * columns,
-        out_shape=[jax.ShapeDtypeStruct((2, TOK, HD), jnp.bfloat16)] * columns,
+        x_refs, o_refs, (x, y) = refs[:blocks], refs[blocks : 2 * blocks], refs[2 * blocks :]
+
+        @pl.when(where_ref[1] == 0)
+        def _():
+            at = [2 * where_ref[0] ^ d for d in range(blocks)]
+            for d in range(blocks):
+                x[at[d]] = x_refs[d][...]
+            sources = [(x, t) for t in range(5)]
+            student_head(range(0, blocks, 2), first_ref[0], sources[:3], y, 0)
+            gen = lambda at: y[at, 0]
+            teacher_head(blocks, range(blocks), clip_ref, sources[3:], gen, y, 1)
+            for d in range(blocks):
+                o_refs[d][...] = y[at[d]]
+
+    return pl.pallas_call(
+        body,
+        in_specs=[SMEM] * 3 + [VMEM] * blocks,
+        out_specs=[VMEM] * blocks,
+        out_shape=[jax.ShapeDtypeStruct((2, TOK, HD), jnp.bfloat16)] * blocks,
         scratch_shapes=[
             pltpu.VMEM((blocks, 5, TOK, HD), jnp.bfloat16),
-            pltpu.VMEM((blocks, 1, TOK, HD), jnp.bfloat16),
+            pltpu.VMEM((blocks, 2, TOK, HD), jnp.bfloat16),
         ],
         compiler_params=LOCAL,
         cost_estimate=cost(2, blocks, 7),
-    )(first, clips, where, *own, *other)
-
-
-def join(base, columns, places, column, back, pieces):
-    def body(column_ref, x_ref, *refs):
-        for i, o_ref in enumerate(refs[columns:]):
+    )(first, clips, where, *arrived)
+
+
+def join(base, columns, places, where, back, pieces):
+    def body(where_ref, x_ref, *refs):
+        column, side = where_ref[0], where_ref[1]
+        for i, o_ref in enumerate(refs[2 * columns :]):
             for h, (p, u) in enumerate(places[i]):
                 o_ref[0, :, h * HD : (h + 1) * HD] = x_ref[p, u]
             for s in range(columns):
-                at = pl.multiple_of((base + (column_ref[0] ^ s)) * HD, HD)
-                o_ref[0, :, pl.ds(at, HD)] = refs[s][i]
+                at = pl.ds(pl.multiple_of((base + (column ^ s)) * HD, HD), HD)
+                o_ref[0, :, at] = jnp.where(side == 0, refs[2 * s][i], refs[2 * s + 1][i])
 
     width = (base + columns) * HD
     return pl.pallas_call(
         body,
-        in_specs=[SMEM, VMEM] + [VMEM] * columns,
+        in_specs=[SMEM, VMEM] + [VMEM] * (2 * columns),
         out_specs=[VMEM] * 2,
         out_shape=[jax.ShapeDtypeStruct((1, TOK, width), jnp.bfloat16)] * 2,
         compiler_params=LOCAL,
         cost_estimate=cost(0, 1, 4 * (base + columns)),
-    )(column, back, *pieces)
+    )(where, back, *pieces)
 
 
 def by_slots_and_columns(tensors, peers, full, rest, first, clips):
     base = full * peers
     here = lax.axis_index("tm")
-    column, side = here // 2, here % 2
-    where = jnp.stack([column, side]).astype(jnp.int32)
-
-    def swapped(x, by):
-        return lax.ppermute(x, "tm", [(i, i ^ by) for i in range(peers)])
+    where = jnp.stack([here // 2, here % 2]).astype(jnp.int32)
+
+    def sent(x, d, home):
+        pairs = [(i, i ^ d) for i in range(peers) if (i if home else i ^ d) % 2 == 0]
+        return lax.ppermute(x, "tm", pairs) if d else x
 
     plan = [[(t, s * peers + p) for s in range(full) for t in range(5)] for p in range(peers)]
     slots = [(s * peers, peers) for s in range(full)]
     arrived = lax.all_to_all(pack(plan, slots, tensors), "tm", 0, 0)
     pieces = rest_pack(base, rest, where[:1], tensors)
-    own = [swapped(x, 2 * s) if s else x for s, x in enumerate(pieces)]
-    other = [swapped(x, 1) for x in own]
-    pieces = rest_kernel(rest, first, clips, where, own, other)
-    arrived, _ = lax.optimization_barrier((arrived, pieces))
+    middle = rest // 2
+    near = [sent(pieces[d // 2], d, False) for d in range(2 * middle)]
+    arrived, far = lax.optimization_barrier((arrived, pieces[middle:]))
+    far = [sent(far[d // 2 - middle], d, False) for d in range(2 * middle, peers)]
     results = slots_kernel(full, peers, first, clips, arrived)
+    results, near, far = lax.optimization_barrier((results, near, far))
     back = lax.all_to_all(results, "tm", 0, 0)
-    pieces = [swapped(x, 2 * s) if s else x for s, x in enumerate(pieces)]
+    pieces = rest_kernel(peers, first, clips, where, near + far)
+    pieces = [sent(x, d, True) for d, x in enumerate(pieces)]
     places = [[(h % peers, 2 * (h // peers) + i) for h in range(base)] for i in (0, 1)]
-    return tuple(join(base, rest, places, where[:1], back, pieces))
+    return tuple(join(base, rest, places, where, back, pieces))
 
 
 def by_roles(tensors, peers, heads, first, clips):

time: 140 us -> 134 us (0.957)
  waiting for transfers between devices: 91.1 us -> 61.3 us
  starting transfers between devices: 26.5 us -> 44.3 us
  local copies, waits for them, and re-layouts: 1.88 us -> 5.73 us
  Pallas kernels: 18.3 us -> 20.1 us
    ppermute x10 -> x14, waiting for transfers between devices: 91 us -> 11.4 us  [sent(): return lax.ppermute(x, 'tm', pairs) if d else x]
    all_to_all x1, waiting for transfers between devices: 0.01 us -> 49.9 us  [by_slots_and_columns(): arrived = lax.all_to_all(pack(plan, slots, tensors), 'tm', 0, 0)]
    ppermute x10 -> x14, starting transfers between devices: 14.5 us -> 30.7 us  [sent(): return lax.ppermute(x, 'tm', pairs) if d else x]
    unnamed x6 -> x18, local copies, waits for them, and re-layouts: 1.88 us -> 5.73 us
    pallas_call x2, Pallas kernels: 4.86 us -> 6.62 us  [the longest x1 4.77 us: rest_kernel(): pl.pallas_call(body, in_specs=[SMEM] * 3 + [VMEM] * blocks, out_specs=[VM...]
    all_to_all x1, starting transfers between devices: 4.77 us -> 6.37 us  [by_slots_and_columns(): back = lax.all_to_all(results, 'tm', 0, 0)]
  transfers between devices with their start and end apart: 12 -> 16, of which waited for: 6 -> 3; matrix products, arithmetic and copies ran while one was open for 0% -> 0% of each run, Pallas kernels for 4% -> 12%
where the time goes in v2:
time: 134 us; the launch traced here: 133 us
  waiting for transfers between devices  61.3 us (46%)
  starting transfers between devices  44.3 us (33%)
  Pallas kernels  20.1 us (15%)
  local copies, waits for them, and re-layouts  5.73 us (4%)
  between operations  1.53 us (1%)
    all_to_all x1, waiting for transfers between devices, by_slots_and_columns(): arrived = lax.all_to_all(pack(plan, slots, tensors), 'tm', 0, 0)  49.9 us
    ppermute x14, starting transfers between devices, sent(): return lax.ppermute(x, 'tm', pairs) if d else x  30.7 us
    ppermute x14, waiting for transfers between devices, sent(): return lax.ppermute(x, 'tm', pairs) if d else x  11.4 us
    pallas_call x1, Pallas kernels, slots_kernel(): pl.pallas_call(body, in_specs=[SMEM, SMEM, VMEM], out_specs=VMEM, out_sha...  8.76 us
    all_to_all x1, starting transfers between devices, by_slots_and_columns(): arrived = lax.all_to_all(pack(plan, slots, tensors), 'tm', 0, 0)  7.26 us
    all_to_all x1, starting transfers between devices, by_slots_and_columns(): back = lax.all_to_all(results, 'tm', 0, 0)  6.37 us
    unnamed x18, local copies, waits for them, and re-layouts  5.73 us
    pallas_call x1, Pallas kernels, rest_kernel(): pl.pallas_call(body, in_specs=[SMEM] * 3 + [VMEM] * blocks, out_specs=[VM...  4.77 us
  transfers between devices with their start and end apart: 16, of which 3 were waited for; matrix products, arithmetic and copies ran while one was open for 0% of the time, Pallas kernels for 12%

profile of v2, /device:TPU:0, one launch (start us, length us, event | category | flops | bytes accessed | tf_op | source)
XLA Modules:
  0.0 133.4 jit_solution(1259338118460513953)
XLA Ops:
  0.6 2.7 %shard_map.86 = bf16[8,10,128,128]{3,2,1,0:T(8,128)(2,1)} custom-call(bf16[1,128,2560]{2,1,0:T(8,128)(2,1)} %refs_0_.3, bf16[1,128,2560]{2,1,0:T(8,128)(2,1)} %refs_1_.3, bf16[1,128,2560]{2,1,0:T(8,128)(2,1)} %refs_2_.3, bf16[1,128,2560]{2,1,0:T(8,128)(2,1)} %refs_3_.3, bf16[1,128,2560]{2,1,0:T(8,128)(2,1)} %refs_4_.3), custom_call_target="tpu_custom_call" | custom-call | bytes 5242880 | tf_op jit(solution)/shard_map/pallas_call | solution.py:112
  3.3 7.3 %all-to-all-start = ((bf16[8,10,128,128]{3,2,1,0:T(8,128)(2,1)}), bf16[8,10,128,128]{3,2,1,0:T(8,128)(2,1)S(1)}, u32[]{:S(2)}, u32[]{:S(2)}) async-start(bf16[8,10,128,128]{3,2,1,0:T(8,128)(2,1)} %shard_map.86), calls=%async_computation | async-start | bytes 5242880 | tf_op jit(solution)/shard_map/all_to_all | solution.py:293
  10.6 0.0 copy-start.8
  10.6 2.1 %shard_map.87 = (bf16[5,128,128]{2,1,0:T(8,128)(2,1)}, bf16[5,128,128]{2,1,0:T(8,128)(2,1)}, bf16[5,128,128]{2,1,0:T(8,128)(2,1)}, bf16[5,128,128]{2,1,0:T(8,128)(2,1)}) custom-call(s32[1]{0:T(128)} %bitcast.column_ref, bf16[1,128,2560]{2,1,0:T(8,128)(2,1)} %refs_0_.3, bf16[1,128,2560]{2,1,0:T(8,128)(2,1)} %refs_1_.3, bf16[1,128,2560]{2,1,0:T(8,128)(2,1)} %refs_2_.3, ...), custom_call_target="tpu_custom_call" | custom-call | bytes 1310720 | tf_op jit(solution)/shard_map/pallas_call | solution.py:217
  12.7 3.9 %collective-permute-start.1 = (bf16[5,128,128]{2,1,0:T(8,128)(2,1)}, bf16[5,128,128]{2,1,0:T(8,128)(2,1)S(1)}, u32[]{:S(2)}, u32[]{:S(2)}) collective-permute-start(bf16[5,128,128]{2,1,0:T(8,128)(2,1)} %get-tuple-element.30), channel_id=1, source_target_pairs={{0,8},{8,0},{16,24},{24,16},{1,9},{9,1},{17,25},{25,17},{2,10},{10... | collective-permute-start | bytes 491528 | tf_op jit(solution)/shard_map/ppermute | solution.py:289
  16.6 1.3 collective-permute-start.2
  17.9 1.3 collective-permute-start
  19.2 0.0 copy-done.8
  19.2 0.2 reduce-window.8
  19.4 0.1 select_reduce_fusion.1
  20.2 49.9 %all-to-all-done.x_ref = bf16[8,10,128,128]{3,2,1,0:T(8,128)(2,1)S(1)} async-done(((bf16[8,10,128,128]{3,2,1,0:T(8,128)(2,1)}), bf16[8,10,128,128]{3,2,1,0:T(8,128)(2,1)S(1)}, u32[]{:S(2)}, u32[]{:S(2)}) %all-to-all-start) | async-done | bytes 2621472 | tf_op jit(solution)/shard_map/all_to_all | solution.py:293
  70.1 0.0 copy-start.1
  70.1 2.0 %collective-permute-start.3 = (bf16[5,128,128]{2,1,0:T(8,128)(2,1)}, bf16[5,128,128]{2,1,0:T(8,128)(2,1)S(1)}, u32[]{:S(2)}, u32[]{:S(2)}) collective-permute-start(bf16[5,128,128]{2,1,0:T(8,128)(2,1)} %get-tuple-element.31), channel_id=1, source_target_pairs={{0,16},{8,24},{16,0},{24,8},{1,17},{9,25},{17,1},{25,9},{2,18},{10... | collective-permute-start | bytes 491528 | tf_op jit(solution)/shard_map/ppermute | solution.py:289
  72.1 1.3 collective-permute-start.4
  73.4 0.0 collective-permute-done.refs_1_
  73.4 4.2 %collective-permute-start.5 = (bf16[5,128,128]{2,1,0:T(8,128)(2,1)}, bf16[5,128,128]{2,1,0:T(8,128)(2,1)S(1)}, u32[]{:S(2)}, u32[]{:S(2)}) collective-permute-start(bf16[5,128,128]{2,1,0:T(8,128)(2,1)} %get-tuple-element.32), channel_id=1, source_target_pairs={{0,24},{8,16},{16,8},{24,0},{1,25},{9,17},{17,9},{25,1},{2,26},{10... | collective-permute-start | bytes 491528 | tf_op jit(solution)/shard_map/ppermute | solution.py:289
  77.6 0.0 collective-permute-done.1.refs_2_
  77.6 1.3 collective-permute-start.6
  78.9 8.8 %shard_map.88 = bf16[8,4,128,128]{3,2,1,0:T(8,128)(2,1)S(1)} custom-call(s32[1]{0:T(128)S(6)} %copy.9.first_ref, s32[2,8]{1,0:T(2,128)S(1)} %pad_add_fusion.clip_ref, bf16[8,10,128,128]{3,2,1,0:T(8,128)(2,1)S(1)} %all-to-all-done.x_ref), custom_call_target="tpu_custom_call" | custom-call | flops 2147483648 | bytes 3670016 | tf_op jit(solution)/shard_map/pallas_call | solution.py:193
  87.7 0.0 copy-start
  87.7 1.0 copy-done
  88.7 0.0 collective-permute-done.2.refs_3_
  88.7 0.0 collective-permute-done.3.refs_4_
  88.7 0.2 collective-permute-done.4.refs_5_
  88.9 0.0 copy-start.2
  88.9 0.7 copy-done.2
  89.6 0.0 collective-permute-done.5.refs_6_
  89.6 0.0 copy-start.4
  89.6 0.7 copy-done.4
  90.3 0.0 collective-permute-done.6.refs_7_
  90.3 0.0 copy-start.6
  90.3 0.7 copy-done.6
  90.9 6.4 %all-to-all-start.1 = ((bf16[8,4,128,128]{3,2,1,0:T(8,128)(2,1)}), bf16[8,4,128,128]{3,2,1,0:T(8,128)(2,1)S(1)}, u32[]{:S(2)}, u32[]{:S(2)}) async-start(bf16[8,4,128,128]{3,2,1,0:T(8,128)(2,1)} %copy-done), calls=%async_computation.1 | async-start | bytes 2097152 | tf_op jit(solution)/shard_map/all_to_all | solution.py:301
  97.3 0.1 pad_add_fusion.1.where_ref
  97.4 0.0 copy-done.1
  97.4 0.0 copy-start.3
  97.4 0.9 copy-done.3
  98.3 0.0 copy-start.5
  98.3 0.9 copy-done.5
  99.2 0.0 copy-start.7
  99.2 0.9 copy-done.7
  100.1 4.8 %shard_map.89 = (bf16[2,128,128]{2,1,0:T(8,128)(2,1)S(1)}, bf16[2,128,128]{2,1,0:T(8,128)(2,1)S(1)}, bf16[2,128,128]{2,1,0:T(8,128)(2,1)S(1)}, bf16[2,128,128]{2...) custom-call(s32[1]{0:T(128)S(6)} %copy.9.first_ref, ...), custom_call_target="tpu_custom_call" | custom-call | flops 1073741824 | bytes 1835008 | tf_op jit(solution)/shard_map/pallas_call | solution.py:247
  104.9 1.3 collective-permute-start.7
  106.2 3.9 %collective-permute-start.8 = (bf16[2,128,128]{2,1,0:T(8,128)(2,1)S(1)}, bf16[2,128,128]{2,1,0:T(8,128)(2,1)S(1)}, u32[]{:S(2)}, u32[]{:S(2)}) collective-permute-start(bf16[2,128,128]{2,1,0:T(8,128)(2,1)S(1)} %get-tuple-element.44), channel_id=1, source_target_pairs={{0,8},{8,0},{16,24},{24,16},{1,9},{9,1},{17,25},{25,17},{2,10},{10... | collective-permute-start | bytes 196616 | tf_op jit(solution)/shard_map/ppermute | solution.py:289
  110.1 1.3 collective-permute-start.9
  111.4 4.3 %collective-permute-start.10 = (bf16[2,128,128]{2,1,0:T(8,128)(2,1)S(1)}, bf16[2,128,128]{2,1,0:T(8,128)(2,1)S(1)}, u32[]{:S(2)}, u32[]{:S(2)}) collective-permute-start(bf16[2,128,128]{2,1,0:T(8,128)(2,1)S(1)} %get-tuple-element.46), channel_id=1, source_target_pairs={{0,16},{8,24},{16,0},{24,8},{1,17},{9,25},{17,1},{25,9},{2,18},{10... | collective-permute-start | bytes 196616 | tf_op jit(solution)/shard_map/ppermute | solution.py:289
  115.7 1.3 collective-permute-start.11
  117.0 0.0 collective-permute-done.7.refs_1_
  117.0 2.0 %collective-permute-start.12 = (bf16[2,128,128]{2,1,0:T(8,128)(2,1)S(1)}, bf16[2,128,128]{2,1,0:T(8,128)(2,1)S(1)}, u32[]{:S(2)}, u32[]{:S(2)}) collective-permute-start(bf16[2,128,128]{2,1,0:T(8,128)(2,1)S(1)} %get-tuple-element.48), channel_id=1, source_target_pairs={{0,24},{8,16},{16,8},{24,0},{1,25},{9,17},{17,9},{25,1},{2,26},{10... | collective-permute-start | bytes 196616 | tf_op jit(solution)/shard_map/ppermute | solution.py:289
  119.0 0.0 collective-permute-done.8.refs_2_
  119.1 1.3 collective-permute-start.13
  120.4 0.0 collective-permute-done.9.refs_3_
  120.4 11.1 %collective-permute-done.10.refs_4_ = bf16[2,128,128]{2,1,0:T(8,128)(2,1)S(1)} collective-permute-done((bf16[2,128,128]{2,1,0:T(8,128)(2,1)S(1)}, bf16[2,128,128]{2,1,0:T(8,128)(2,1)S(1)}, u32[]{:S(2)}, u32[]{:S(2)}) %collective-permute-start.10) | collective-permute-done | bytes 65568 | tf_op jit(solution)/shard_map/ppermute | solution.py:289
  131.5 0.0 collective-permute-done.11.refs_5_
  131.5 0.0 collective-permute-done.12.refs_6_
  131.5 0.0 collective-permute-done.13.refs_7_
  131.5 0.0 all-to-all-done.1.x_ref
  131.5 1.8 %shard_map.90 = (bf16[1,128,2560]{2,1,0:T(8,128)(2,1)}, bf16[1,128,2560]{2,1,0:T(8,128)(2,1)}) custom-call(s32[2]{0:T(128)S(1)} %pad_add_fusion.1.where_ref, bf16[8,4,128,128]{3,2,1,0:T(8,128)(2,1)S(1)} %all-to-all-done.1.x_ref, bf16[2,128,128]{2,1,0:T(8,128)(2,1)S(1)} %get-tuple-element.42.refs_0_, bf16[2,128,128]{2,1,0:T(8,128)(2,1)S(1)} %collective-permute-done.7.refs_1_, ...), custom_call_target="tpu_custom_call" | custom-call | bytes 2621440 | tf_op jit(solution)/shard_map/pallas_call | solution.py:272
  (1 shorter events, 0.0 us)
Async XLA Ops:
  3.3 66.7 %all-to-all-start = ((bf16[8,10,128,128]{3,2,1,0:T(8,128)(2,1)}), bf16[8,10,128,128]{3,2,1,0:T(8,128)(2,1)S(1)}, u32[]{:S(2)}, u32[]{:S(2)}) async-start(bf16[8,10,128,128]{3,2,1,0:T(8,128)(2,1)} %shard_map.86), calls=%async_computation | async-start | bytes 5242880 | tf_op jit(solution)/shard_map/all_to_all | solution.py:293
  10.6 8.6 %copy-start.8 = (s32[1,3]{1,0:T(1,128)S(1)}, s32[1,3]{1,0:T(1,128)}, u32[]{:S(2)}) copy-start(s32[1,3]{1,0:T(1,128)} %param.13) | copy-start | bytes 40
  12.7 64.9 %collective-permute-start.1 = (bf16[5,128,128]{2,1,0:T(8,128)(2,1)}, bf16[5,128,128]{2,1,0:T(8,128)(2,1)S(1)}, u32[]{:S(2)}, u32[]{:S(2)}) collective-permute-start(bf16[5,128,128]{2,1,0:T(8,128)(2,1)} %get-tuple-element.30), channel_id=1, source_target_pairs={{0,8},{8,0},{16,24},{24,16},{1,9},{9,1},{17,25},{25,17},{2,10},{10... | collective-permute-start | bytes 491528 | tf_op jit(solution)/shard_map/ppermute | solution.py:289
  16.6 72.1 %collective-permute-start.2 = (bf16[5,128,128]{2,1,0:T(8,128)(2,1)}, bf16[5,128,128]{2,1,0:T(8,128)(2,1)S(1)}, u32[]{:S(2)}, u32[]{:S(2)}) collective-permute-start(bf16[5,128,128]{2,1,0:T(8,128)(2,1)} %get-tuple-element.30), channel_id=1, source_target_pairs={{4,8},{12,0},{20,24},{28,16},{5,9},{13,1},{21,25},{29,17},{6,10},{... | collective-permute-start | bytes 491528 | tf_op jit(solution)/shard_map/ppermute | solution.py:289
  17.9 55.5 %collective-permute-start = (bf16[5,128,128]{2,1,0:T(8,128)(2,1)}, bf16[5,128,128]{2,1,0:T(8,128)(2,1)S(1)}, u32[]{:S(2)}, u32[]{:S(2)}) collective-permute-start(bf16[5,128,128]{2,1,0:T(8,128)(2,1)} %get-tuple-element.34.refs_0_), channel_id=1, source_target_pairs={{4,0},{12,8},{20,16},{28,24},{5,1},{13,9},{21,17},{29,25},{6,2},{1... | collective-permute-start | bytes 491528 | tf_op jit(solution)/shard_map/ppermute | solution.py:289
  70.1 27.3 %copy-start.1 = (bf16[5,128,128]{2,1,0:T(8,128)(2,1)S(1)}, bf16[5,128,128]{2,1,0:T(8,128)(2,1)}, u32[]{:S(2)}) copy-start(bf16[5,128,128]{2,1,0:T(8,128)(2,1)} %get-tuple-element.34.refs_0_) | copy-start | bytes 491524
  70.1 18.6 %collective-permute-start.3 = (bf16[5,128,128]{2,1,0:T(8,128)(2,1)}, bf16[5,128,128]{2,1,0:T(8,128)(2,1)S(1)}, u32[]{:S(2)}, u32[]{:S(2)}) collective-permute-start(bf16[5,128,128]{2,1,0:T(8,128)(2,1)} %get-tuple-element.31), channel_id=1, source_target_pairs={{0,16},{8,24},{16,0},{24,8},{1,17},{9,25},{17,1},{25,9},{2,18},{10... | collective-permute-start | bytes 491528 | tf_op jit(solution)/shard_map/ppermute | solution.py:289
  72.1 16.8 %collective-permute-start.4 = (bf16[5,128,128]{2,1,0:T(8,128)(2,1)}, bf16[5,128,128]{2,1,0:T(8,128)(2,1)S(1)}, u32[]{:S(2)}, u32[]{:S(2)}) collective-permute-start(bf16[5,128,128]{2,1,0:T(8,128)(2,1)} %get-tuple-element.31), channel_id=1, source_target_pairs={{4,16},{12,24},{20,0},{28,8},{5,17},{13,25},{21,1},{29,9},{6,18},{... | collective-permute-start | bytes 491528 | tf_op jit(solution)/shard_map/ppermute | solution.py:289
  73.4 16.2 %collective-permute-start.5 = (bf16[5,128,128]{2,1,0:T(8,128)(2,1)}, bf16[5,128,128]{2,1,0:T(8,128)(2,1)S(1)}, u32[]{:S(2)}, u32[]{:S(2)}) collective-permute-start(bf16[5,128,128]{2,1,0:T(8,128)(2,1)} %get-tuple-element.32), channel_id=1, source_target_pairs={{0,24},{8,16},{16,8},{24,0},{1,25},{9,17},{17,9},{25,1},{2,26},{10... | collective-permute-start | bytes 491528 | tf_op jit(solution)/shard_map/ppermute | solution.py:289
  77.6 12.6 %collective-permute-start.6 = (bf16[5,128,128]{2,1,0:T(8,128)(2,1)}, bf16[5,128,128]{2,1,0:T(8,128)(2,1)S(1)}, u32[]{:S(2)}, u32[]{:S(2)}) collective-permute-start(bf16[5,128,128]{2,1,0:T(8,128)(2,1)} %get-tuple-element.32), channel_id=1, source_target_pairs={{4,24},{12,16},{20,8},{28,0},{5,25},{13,17},{21,9},{29,1},{6,26},{... | collective-permute-start | bytes 491528 | tf_op jit(solution)/shard_map/ppermute | solution.py:289
  87.7 1.0 copy-start
  88.9 0.7 copy-start.2
  89.6 0.7 copy-start.4
  90.3 0.7 copy-start.6
  90.9 40.6 %all-to-all-start.1 = ((bf16[8,4,128,128]{3,2,1,0:T(8,128)(2,1)}), bf16[8,4,128,128]{3,2,1,0:T(8,128)(2,1)S(1)}, u32[]{:S(2)}, u32[]{:S(2)}) async-start(bf16[8,4,128,128]{3,2,1,0:T(8,128)(2,1)} %copy-done), calls=%async_computation.1 | async-start | bytes 2097152 | tf_op jit(solution)/shard_map/all_to_all | solution.py:301
  97.4 0.9 copy-start.3
  98.3 0.9 copy-start.5
  99.2 0.9 copy-start.7
  104.9 12.1 %collective-permute-start.7 = (bf16[2,128,128]{2,1,0:T(8,128)(2,1)S(1)}, bf16[2,128,128]{2,1,0:T(8,128)(2,1)S(1)}, u32[]{:S(2)}, u32[]{:S(2)}) collective-permute-start(bf16[2,128,128]{2,1,0:T(8,128)(2,1)S(1)} %get-tuple-element.43), channel_id=1, source_target_pairs={{0,4},{8,12},{16,20},{24,28},{1,5},{9,13},{17,21},{25,29},{2,6},{1... | collective-permute-start | bytes 196616 | tf_op jit(solution)/shard_map/ppermute | solution.py:289
  106.2 12.9 %collective-permute-start.8 = (bf16[2,128,128]{2,1,0:T(8,128)(2,1)S(1)}, bf16[2,128,128]{2,1,0:T(8,128)(2,1)S(1)}, u32[]{:S(2)}, u32[]{:S(2)}) collective-permute-start(bf16[2,128,128]{2,1,0:T(8,128)(2,1)S(1)} %get-tuple-element.44), channel_id=1, source_target_pairs={{0,8},{8,0},{16,24},{24,16},{1,9},{9,1},{17,25},{25,17},{2,10},{10... | collective-permute-start | bytes 196616 | tf_op jit(solution)/shard_map/ppermute | solution.py:289
  110.1 10.2 %collective-permute-start.9 = (bf16[2,128,128]{2,1,0:T(8,128)(2,1)S(1)}, bf16[2,128,128]{2,1,0:T(8,128)(2,1)S(1)}, u32[]{:S(2)}, u32[]{:S(2)}) collective-permute-start(bf16[2,128,128]{2,1,0:T(8,128)(2,1)S(1)} %get-tuple-element.45), channel_id=1, source_target_pairs={{0,12},{8,4},{16,28},{24,20},{1,13},{9,5},{17,29},{25,21},{2,14},{... | collective-permute-start | bytes 196616 | tf_op jit(solution)/shard_map/ppermute | solution.py:289
  111.4 20.1 %collective-permute-start.10 = (bf16[2,128,128]{2,1,0:T(8,128)(2,1)S(1)}, bf16[2,128,128]{2,1,0:T(8,128)(2,1)S(1)}, u32[]{:S(2)}, u32[]{:S(2)}) collective-permute-start(bf16[2,128,128]{2,1,0:T(8,128)(2,1)S(1)} %get-tuple-element.46), channel_id=1, source_target_pairs={{0,16},{8,24},{16,0},{24,8},{1,17},{9,25},{17,1},{25,9},{2,18},{10... | collective-permute-start | bytes 196616 | tf_op jit(solution)/shard_map/ppermute | solution.py:289
  115.7 15.8 %collective-permute-start.11 = (bf16[2,128,128]{2,1,0:T(8,128)(2,1)S(1)}, bf16[2,128,128]{2,1,0:T(8,128)(2,1)S(1)}, u32[]{:S(2)}, u32[]{:S(2)}) collective-permute-start(bf16[2,128,128]{2,1,0:T(8,128)(2,1)S(1)} %get-tuple-element.47), channel_id=1, source_target_pairs={{0,20},{8,28},{16,4},{24,12},{1,21},{9,29},{17,5},{25,13},{2,22},{... | collective-permute-start | bytes 196616 | tf_op jit(solution)/shard_map/ppermute | solution.py:289
  117.0 14.5 %collective-permute-start.12 = (bf16[2,128,128]{2,1,0:T(8,128)(2,1)S(1)}, bf16[2,128,128]{2,1,0:T(8,128)(2,1)S(1)}, u32[]{:S(2)}, u32[]{:S(2)}) collective-permute-start(bf16[2,128,128]{2,1,0:T(8,128)(2,1)S(1)} %get-tuple-element.48), channel_id=1, source_target_pairs={{0,24},{8,16},{16,8},{24,0},{1,25},{9,17},{17,9},{25,1},{2,26},{10... | collective-permute-start | bytes 196616 | tf_op jit(solution)/shard_map/ppermute | solution.py:289
  119.1 12.5 %collective-permute-start.13 = (bf16[2,128,128]{2,1,0:T(8,128)(2,1)S(1)}, bf16[2,128,128]{2,1,0:T(8,128)(2,1)S(1)}, u32[]{:S(2)}, u32[]{:S(2)}) collective-permute-start(bf16[2,128,128]{2,1,0:T(8,128)(2,1)S(1)} %get-tuple-element.49), channel_id=1, source_target_pairs={{0,28},{8,20},{16,12},{24,4},{1,29},{9,21},{17,13},{25,5},{2,30},{... | collective-permute-start | bytes 196616 | tf_op jit(solution)/shard_map/ppermute | solution.py:289
